TPU v7x, 1024 devices: a whole 8x8x8 slice. The times are simulated.
1024 devices in a mesh: replica: 4 (over y_lo), fsdp: 256 (over y_hi, x, z, core).
Axes of the slice: x: 8, y: 8 (y_hi: 2, y_lo: 4; y = y_hi * 4 + y_lo), z: 8, core: 2. Of those that a mesh axis runs over, the one named last changes fastest.
Arguments:
- delta_codes: int32 [4, 8192, 128], P('replica', 'fsdp'), may hold values from 0 to 15
- scale_exponents: int32 [4, 8192, 4], P('replica', 'fsdp'), may hold values from -6 to -3
- error_feedback: float32 [4, 8192, 128], P('replica', 'fsdp'), may hold values from -0.3 to 0.3
- base_weights: float32 [8192, 128], P('fsdp'), may hold values from -5 to 5
- outer_momentum: float32 [8192, 128], P('fsdp'), may hold values from -1.2 to 1.2
- norm_gain: float32 [8192], replicated, may hold values from 0.1 to 1.9
- hidden_states: bfloat16 [4, 49152, 8192], P('replica', 'fsdp'), may hold values from -24 to 24
- key_cotangent: bfloat16 [4, 49152, 128], P('replica', 'fsdp'), may hold values from -8 to 8
Outputs:
- projected: bfloat16 [4, 49152, 128], P('replica', 'fsdp')
- weight_grad: float32 [4, 8192, 128], P('replica', 'fsdp')
- new_weights: float32 [8192, 128], P('fsdp')
- new_momentum: float32 [8192, 128], P('fsdp')
All inputs are finite; a program needn't handle non-finite values.
Results may differ from a plain program's by a relative error of at most 0.0057.
Values may be sent and summed in bfloat16 or wider, within the bound.
A program may use at most 32 MiB of HBM per device.

v0:
```python
import math

import jax
import jax.numpy as jnp
from jax import lax
from jax.sharding import PartitionSpec as P

BLOCK = 32


def decode(delta_codes, scale_exponents):
    polarity = jnp.where(delta_codes >= 8, 1.0, 0.0).astype(jnp.float32)
    polarity = 1.0 - 2.0 * polarity
    mantissa_code = delta_codes % 8
    exponent = mantissa_code // 2
    fraction = (mantissa_code % 2).astype(jnp.float32)
    magnitude = jnp.where(
        exponent == 0,
        0.5 * fraction,
        jnp.exp2((exponent - 1).astype(jnp.float32)) * (1.0 + 0.5 * fraction),
    )
    multiplier = jnp.exp2(scale_exponents.astype(jnp.float32))
    extent = delta_codes.shape
    blocked = (polarity * magnitude).reshape(extent[:-1] + (extent[-1] // BLOCK, BLOCK))
    return (blocked * multiplier[..., None]).reshape(extent)


def nesterov(outer_grad, base_weights, outer_momentum):
    new_momentum = 0.9 * outer_momentum + outer_grad
    new_weights = base_weights - 0.7 * (outer_grad + 0.9 * new_momentum)
    return (new_momentum, new_weights)


def rms_normed(hidden_block, norm_gain):
    widened = hidden_block.astype(jnp.float32)
    inverse = lax.rsqrt(jnp.mean(widened * widened, axis=-1, keepdims=True) + 1e-05)
    return (widened * inverse * norm_gain).astype(jnp.bfloat16)


def shards(
    delta_codes,
    scale_exponents,
    error_feedback,
    base_weights,
    outer_momentum,
    norm_gain,
    hidden_states,
    key_cotangent,
):
    replicas = lax.axis_size("replica")
    model_width = hidden_states.shape[2]
    multiplier = 1.0 / math.sqrt(model_width)
    local_term = jnp.sum(decode(delta_codes, scale_exponents) + error_feedback, axis=0)
    normed = rms_normed(hidden_states[0], norm_gain)
    cotangent = key_cotangent[0]
    summed = lax.psum(local_term, "replica")
    new_momentum, new_weights = nesterov(summed / replicas, base_weights, outer_momentum)
    weight_rows = new_weights.astype(jnp.bfloat16)
    columns = normed
    key_sums = jnp.dot(
        columns,
        lax.all_gather(weight_rows, "fsdp", axis=0, tiled=True),
        preferred_element_type=jnp.float32,
    )
    projected = (key_sums * multiplier).astype(jnp.bfloat16)
    columns = normed
    product = lax.dot_general(
        columns, cotangent, (((0,), (0,)), ((), ())), preferred_element_type=jnp.float32
    )
    weight_grad = lax.psum_scatter(product * multiplier, "fsdp", scatter_dimension=0, tiled=True)
    return (projected[None], weight_grad[None], new_weights, new_momentum)


def solution(mesh):
    return jax.shard_map(
        shards,
        mesh=mesh,
        in_specs=(
            P("replica", "fsdp", None),
            P("replica", "fsdp", None),
            P("replica", "fsdp", None),
            P("fsdp", None),
            P("fsdp", None),
            P(),
            P("replica", "fsdp", None),
            P("replica", "fsdp", None),
        ),
        out_specs=(
            P("replica", "fsdp", None),
            P("replica", "fsdp", None),
            P("fsdp", None),
            P("fsdp", None),
        ),
        check_vma=False,
    )
```

profile of v0, /device:TPU:1, one launch (start us, length us, event | category | flops | bytes accessed | tf_op | source)
XLA Modules:
  0.0 1794.8 jit_solution(11225869414617849162)
XLA Ops:
  7.2 0.0 copy-start
  7.2 0.0 all-gather.2.cloned.1.call-start
  7.2 0.7 exponential_bitcast_fusion
  7.9 0.1 copy.12
  8.0 0.1 mul.95
  8.1 0.1 mul.96
  8.2 0.8 add_bitcast_fusion
  9.0 16.4 psum.7
  25.4 1.4 fusion.29
  26.7 0.0 all-gather.2.cloned.1.call-update
  26.8 0.0 reduce-scatter.2.cloned.1.call-start
  26.8 2.6 fusion.2
  29.4 0.0 copy-done
  29.4 5.3 convolution_multiply_fusion
  34.8 0.0 copy-start.1
  34.8 0.0 copy-start.2
  34.8 0.0 reduce-scatter.2.cloned.1.call-update
  34.8 137.4 %all-gather.2.cloned.1.call-done = bf16[8192,128]{1,0:T(8,128)(2,1)} async-done(((bf16[32,128]{1,0:T(8,128)(2,1)}), bf16[8192,128]{1,0:T(8,128)(2,1)}) %all-gather.2.cloned.1.call-update) | async-done | bytes 2097168 | tf_op jit(solution)/shard_map/all_gather | solution.py:62
  172.2 0.0 copy-done.1
  172.2 0.0 copy-done.2
  172.2 3.4 fusion.21
  175.6 1612.4 %reduce-scatter.2.cloned.1.call-done = f32[32,128]{1,0:T(8,128)} async-done(((f32[8192,128]{1,0:T(8,128)}), f32[32,128]{1,0:T(8,128)}) %reduce-scatter.2.cloned.1.call-update) | async-done | bytes 16400 | tf_op jit(solution)/shard_map/reduce_scatter | solution.py:70
  (1 shorter events, 0.0 us)
Async XLA Ops:
  7.2 22.3 %copy-start = (bf16[1,192,128]{2,1,0:T(8,128)(2,1)S(1)}, bf16[1,192,128]{2,1,0:T(8,128)(2,1)}, u32[]{:S(2)}) copy-start(bf16[1,192,128]{2,1,0:T(8,128)(2,1)} %param.15) | copy-start | bytes 147460
  7.2 165.0 %all-gather.2.cloned.1.call-start = ((), (), s32[]{:S(2)}) async-start(), calls=%async_computation.1 | async-start | bytes 2105344 | tf_op jit(solution)/shard_map/all_gather | solution.py:62
  26.8 1761.2 %reduce-scatter.2.cloned.1.call-start = ((), (), s32[]{:S(2)}) async-start(), calls=%async_computation.2 | async-start | bytes 4210688 | tf_op jit(solution)/shard_map/reduce_scatter | solution.py:70
  34.8 137.5 %copy-start.1 = (bf16[1,192,8192]{2,1,0:T(8,128)(2,1)S(1)}, bf16[1,192,8192]{2,1,0:T(8,128)(2,1)}, u32[]{:S(2)}) copy-start(bf16[1,192,8192]{2,1,0:T(8,128)(2,1)} %param.14) | copy-start | bytes 9437188
  34.8 137.5 %copy-start.2 = (f32[8192]{0:T(1024)S(1)}, f32[8192]{0:T(1024)}, u32[]{:S(2)}) copy-start(f32[8192]{0:T(1024)} %param.13) | copy-start | bytes 98308
Sparse Core Ops, SparseCore 0:
  26.9 145.2 all-gather.1
  176.2 1611.7 reduce-scatter.1
where the time goes:
time: 1800 us; the launch traced here: 1790 us
  waiting for transfers between devices  1750 us (97%)
    reduce_scatter x1, waiting for transfers between devices, shards(): lax.psum_scatter(product * multiplier, 'fsdp', scatter_dimension=0, tiled...  1610 us
    all_gather x1, waiting for transfers between devices, shards(): lax.all_gather(weight_rows, 'fsdp', axis=0, tiled=True)  137 us
  transfers between devices with their start and end apart: 2, of which 2 were waited for; matrix products, arithmetic and copies ran while one was open for 1% of the time, Pallas kernels for 0%

commit v1 on v0

v1 whole, which is shorter than its diff:
```python
import functools
import math

import jax
import jax.numpy as jnp
from jax import lax
from jax.experimental import pallas as pl
from jax.experimental.pallas import tpu as pltpu
from jax.sharding import PartitionSpec as P

BLOCK = 32
ROWS = 32
PAIR = 2 * ROWS
LANES = 128
NQ = 2
NG = 2
NX = 4
MESH = pl.DeviceIdType.MESH
BF16 = jnp.bfloat16
F32 = jnp.float32


def decode(codes, exponents):
    lane = lax.broadcasted_iota(jnp.int32, codes.shape, 1)
    exponent = jnp.zeros(codes.shape, jnp.int32)
    for k in range(codes.shape[1] // BLOCK):
        exponent = jnp.where(lane // BLOCK == k, exponents[:, k : k + 1], exponent)
    scale = jnp.where(
        exponent == -6,
        2.0**-6,
        jnp.where(exponent == -5, 2.0**-5, jnp.where(exponent == -4, 2.0**-4, 2.0**-3)),
    ).astype(F32)
    magnitude_code = codes % 8
    level = magnitude_code // 2
    fraction = 0.5 * (magnitude_code % 2).astype(F32)
    magnitude = jnp.where(
        level == 0,
        fraction,
        jnp.where(level == 1, 1.0, jnp.where(level == 2, 2.0, 4.0)).astype(F32)
        * (1.0 + fraction),
    )
    return jnp.where(codes >= 8, -magnitude, magnitude) * scale


def kernel(
    replicas,
    n,
    tokens,
    codes_hbm,
    exps_hbm,
    err_hbm,
    base_hbm,
    mom_hbm,
    gain_hbm,
    hidden_hbm,
    cot_hbm,
    proj_ref,
    grad_ref,
    neww_ref,
    newm_ref,
    codes,
    exps,
    err,
    base,
    mom,
    gain,
    cot,
    hid,
    hother,
    cots,
    terms,
    wrows,
    wh,
    prod,
    total,
    rs_out,
    rs_in,
    rs2_out,
    rs2_in,
    rs3_out,
    rs3_in,
    part_out,
    part_in,
    load_sem,
    term_send,
    term_recv,
    hx_send,
    hx_recv,
    cx_sem,
    wy_send,
    wy_recv,
    ag1_send,
    ag1_recv,
    ag2_send,
    ag2_recv,
    rs_send,
    rs_recv,
    rs2_send,
    rs2_recv,
    rs3_send,
    rs3_recv,
    part_sem,
):
    half = n * n * PAIR
    h = n // 2
    model_width = 2 * half
    multiplier = 1.0 / math.sqrt(model_width)
    r = lax.axis_index("replica")
    index = lax.axis_index("fsdp")
    c = index % 2
    z = (index // 2) % n
    x = (index // (2 * n)) % n
    yh = index // (2 * n * n)
    me_a = (1 - c) * z + c * x
    me_b = (1 - c) * x + c * z

    def device(y_half, a, b):
        to_x = (1 - c) * b + c * a
        to_z = (1 - c) * a + c * b
        return (r, ((y_half * n + to_x) * n + to_z) * 2 + c)

    def on_chip(y_half, core):
        return (r, ((y_half * n + x) * n + z) * 2 + core)

    def along_a(step):
        return device(yh, lax.rem(me_a + step + n, n), me_b)

    def along_b(step):
        return device(yh, me_a, lax.rem(me_b + step + n, n))

    sibling = on_chip(yh, 1 - c)

    own = pl.ds(pl.multiple_of(c * half, half), half)
    others = pl.ds(pl.multiple_of((1 - c) * half, half), half)
    small = [
        (codes_hbm, codes),
        (exps_hbm, exps),
        (err_hbm, err),
        (base_hbm, base),
        (mom_hbm, mom),
        (gain_hbm, gain),
        (cot_hbm, cot),
    ]
    loads = [
        pltpu.make_async_copy(src, dst, load_sem.at[i])
        for i, (src, dst) in enumerate(small)
    ]
    load_own = pltpu.make_async_copy(
        hidden_hbm.at[:, own], hid.at[pl.ds(0, tokens)], load_sem.at[len(small)]
    )
    load_other = pltpu.make_async_copy(
        hidden_hbm.at[:, others], hother, load_sem.at[len(small) + 1]
    )

    barrier = pltpu.get_barrier_semaphore()
    partners = [(lax.rem(r + d, replicas), index) for d in range(1, replicas)]
    partners += [sibling, on_chip(1 - yh, 0), on_chip(1 - yh, 1)]
    partners += [along_a(d) for d in range(1, n)]
    partners += [along_b(d) for d in range(1, n)]
    for partner in partners:
        pl.semaphore_signal(barrier, inc=1, device_id=partner, device_id_type=MESH)
    for load in loads:
        load.start()
    load_own.start()
    load_other.start()

    for load in loads[:3]:
        load.wait()
    terms[r] = decode(codes[...], exps[...]) + err[...]
    for load in loads[3:]:
        load.wait()
    flat = index * ROWS
    gain_row = gain[pl.ds(flat // LANES, 1), :]
    lane = lax.broadcasted_iota(jnp.int32, (ROWS, LANES), 1)
    row = lax.broadcasted_iota(jnp.int32, (ROWS, LANES), 0)
    gain_col = jnp.sum(
        jnp.where(lane == row + lax.rem(flat, LANES), gain_row, 0.0),
        axis=1,
        keepdims=True,
    )

    pl.semaphore_wait(barrier, len(partners))

    def remote(src, dst, send, recv, to):
        return pltpu.make_async_remote_copy(
            src_ref=src,
            dst_ref=dst,
            send_sem=send,
            recv_sem=recv,
            device_id=to,
            device_id_type=MESH,
        )

    term_copies = []
    for d in range(1, replicas):
        copy = remote(
            terms.at[r],
            terms.at[r],
            term_send.at[d],
            term_recv.at[d],
            (lax.rem(r + d, replicas), index),
        )
        copy.start()
        term_copies.append(copy)
    hx_copies = []
    piece = tokens // NX
    for i in range(NX):
        copy = remote(
            hidden_hbm.at[pl.ds(i * piece, piece), others],
            hid.at[pl.ds(tokens + i * piece, piece)],
            hx_send.at[i],
            hx_recv.at[i],
            sibling,
        )
        copy.start()
        hx_copies.append(copy)

    load_own.wait()
    load_other.wait()
    inverse = []
    for g in range(tokens // 16):
        rows = pl.ds(g * 16, 16)
        square = jnp.zeros((16, LANES), F32)
        for ref in (hid, hother):
            for j in range(half // LANES):
                wide = ref[rows, j * LANES : (j + 1) * LANES].astype(F32)
                square = square + wide * wide
        mean = jnp.sum(square, axis=1, keepdims=True) * (1.0 / model_width)
        inv = lax.rsqrt(mean + 1e-05)
        inverse.append(inv)
        cots[rows, :] = (cot[rows, :].astype(F32) * inv).astype(BF16)
    cx_copy = remote(
        cots.at[pl.ds(0, tokens)],
        cots.at[pl.ds(tokens, tokens)],
        cx_sem.at[0],
        cx_sem.at[1],
        sibling,
    )
    cx_copy.start()

    for copy in term_copies:
        copy.wait_recv()
    summed = terms[0]
    for d in range(1, replicas):
        summed = summed + terms[d]
    outer_grad = summed / replicas
    new_momentum = 0.9 * mom[...] + outer_grad
    new_weights = base[...] - 0.7 * (outer_grad + 0.9 * new_momentum)
    newm_ref[...] = new_momentum
    neww_ref[...] = new_weights
    scaled_rows = (new_weights * gain_col).astype(BF16)
    wrows[...] = scaled_rows

    core_a = (1 - yh) * z + yh * x
    core_b = (1 - yh) * x + yh * z
    place = wh.at[core_b, core_a, pl.ds(pl.multiple_of(c * ROWS, ROWS), ROWS)]
    wy_far = remote(wrows, place, wy_send.at[0], wy_recv.at[c], on_chip(1 - yh, yh))
    wy_near = remote(wrows, place, wy_send.at[1], wy_recv.at[c], sibling)
    wy_far.start()

    @pl.when(c != yh)
    def _():
        wy_near.start()

    @pl.when(c == yh)
    def _():
        wh[core_b, core_a, pl.ds(pl.multiple_of(c * ROWS, ROWS), ROWS)] = scaled_rows

    def wy_wait(core):
        spot = wh.at[me_b, me_a, pl.ds(pl.multiple_of(core * ROWS, ROWS), ROWS)]
        remote(wrows, spot, wy_send.at[0], wy_recv.at[core], sibling).wait_recv()

    for copy in hx_copies:
        copy.wait_recv()
    cx_copy.wait_recv()
    cots_t = cots[...].T
    my_pair = me_a // 2

    def products(offset):
        p = lax.rem(my_pair + offset, h)
        for j in range(0, n, 2):
            tiles = []
            for t in (j, j + 1):
                at = (1 - c) * (t * n * PAIR + p * LANES) + c * (
                    p * 2 * n * PAIR + t * LANES
                )
                tiles.append(hid[:, pl.ds(pl.multiple_of(at, LANES), LANES)])
            out = jnp.dot(
                cots_t,
                jnp.concatenate(tiles, axis=1),
                preferred_element_type=F32,
            ).T
            for i, t in enumerate((j, j + 1)):
                for s in range(2):
                    a = 2 * p + (1 - c) * s + c * (t // h)
                    b = (1 - c) * t + c * (2 * (t % h) + s)
                    start = i * LANES + s * PAIR
                    prod[a, b] = out[start : start + PAIR]

    order = sorted(range(n), key=lambda d: -min(d, n - d))
    groups = [order[q * n // NQ : (q + 1) * n // NQ] for q in range(NQ)]
    rs_slots = {}
    for q in range(NQ):
        for k in range(h):
            for way in range(2):
                if k > 0 or way == 0:
                    rs_slots[q, way, k] = len(rs_slots)

    def rs_copy(q, way, k):
        slot = rs_slots[q, way, k]
        direction = 1 if (q + way) % 2 == 0 else -1
        return direction, remote(
            rs_out.at[slot],
            rs_in.at[slot],
            rs_send.at[slot],
            rs_recv.at[slot],
            along_a(direction),
        )

    def rs_step(k):
        for way in range(2):
            for q in range(NQ):
                if (q, way, k) not in rs_slots:
                    continue
                slot = rs_slots[q, way, k]
                direction, copy = rs_copy(q, way, k)
                to = lax.rem(me_a + direction * (h - k) + n, n)
                before = rs_slots.get((q, way, k - 1))
                if before is not None:
                    rs_copy(q, way, k - 1)[1].wait_recv()
                for i, d in enumerate(groups[q]):
                    value = prod[to, lax.rem(me_b + d, n)]
                    if before is not None:
                        value = value + rs_in[before, i].astype(F32)
                    rs_out[slot, i] = value.astype(BF16)
                copy.start()

    def rs2_copy(d):
        return remote(
            rs2_out.at[d], rs2_in.at[d], rs2_send.at[d], rs2_recv.at[d], along_b(d)
        )

    def rs_last(q):
        for way in range(2):
            if (q, way, h - 1) in rs_slots:
                rs_copy(q, way, h - 1)[1].wait_recv()
        for i, d in enumerate(groups[q]):
            value = prod[me_a, lax.rem(me_b + d, n)]
            for way in range(2):
                slot = rs_slots.get((q, way, h - 1))
                if slot is not None:
                    value = value + rs_in[slot, i].astype(F32)
            if d == 0:
                total[...] = value
            else:
                rs2_out[d] = value.astype(BF16)
                rs2_copy(d).start()

    def ag1_copy(d):
        spot = wh.at[me_b, me_a]
        return remote(spot, spot, ag1_send.at[d], ag1_recv.at[d], along_a(d))

    def ag1_wait(d):
        spot = wh.at[me_b, lax.rem(me_a - d + n, n)]
        remote(spot, spot, ag1_send.at[d], ag1_recv.at[d], along_a(d)).wait_recv()

    ag_slots = {}
    for q in range(NG):
        for k in range(h):
            for way in range(2):
                if k < h - 1 or way == 0:
                    ag_slots[q, way, k] = len(ag_slots)

    def ag_copy(q, way, k, received=False):
        slot = ag_slots[q, way, k]
        direction = 1 if (q + way) % 2 == 0 else -1
        back = k + 1 if received else k
        b = lax.rem(me_b - direction * back + n, n)
        spot = wh.at[b, pl.ds(q * n // NG, n // NG)]
        return remote(
            spot, spot, ag2_send.at[slot], ag2_recv.at[slot], along_b(direction)
        )

    def ag_step(k):
        for way in range(2):
            for q in range(NG):
                if (q, way, k - 1) in ag_slots:
                    ag_copy(q, way, k - 1, received=True).wait_recv()
                if (q, way, k) in ag_slots:
                    ag_copy(q, way, k).start()

    pairs = sorted(range(h), key=lambda d: -min(d, h - d))
    products(pairs[0])
    rs_step(0)
    wy_wait(1 - c)

    @pl.when(c != yh)
    def _():
        wy_wait(c)

    for d in order[:-1]:
        ag1_copy(d).start()
    for offset in pairs[1:]:
        products(offset)
    for k in range(1, h + 1):
        if k < h:
            rs_step(k)
        if k == 1:
            for d in order[:-1]:
                ag1_wait(d)
        ag_step(k - 1)
    for q in range(NQ):
        rs_last(q)
    ag_step(h)

    pieces = []
    for tx in range(n):
        for tz in range(n):
            pieces.append(wh[(1 - c) * tx + c * tz, (1 - c) * tz + c * tx])
    partial = jnp.dot(
        hid[...], jnp.concatenate(pieces, axis=0), preferred_element_type=F32
    )
    part_out[...] = partial[tokens:]
    part_copy = remote(part_out, part_in, part_sem.at[0], part_sem.at[1], sibling)
    part_copy.start()

    summed = total[...]
    for d in order[:-1]:
        rs2_copy(d).wait_recv()
        summed = summed + rs2_in[d].astype(F32)

    upper = summed[:ROWS]
    lower = summed[ROWS:]
    rs3_out[0] = upper
    rs3_out[1] = lower
    near = remote(
        rs3_out.at[1 - c], rs3_in.at[0], rs3_send.at[1 - c], rs3_recv.at[0], sibling
    )
    far = [
        remote(
            rs3_out.at[core],
            rs3_in.at[1],
            rs3_send.at[core],
            rs3_recv.at[1],
            on_chip(1 - yh, core),
        )
        for core in range(2)
    ]

    @pl.when(c == yh)
    def _():
        near.start()
        rs3_in[0] = rs3_out[c]

    @pl.when(c != yh)
    def _():
        far[0].start()
        far[1].start()

    part_copy.wait_recv()
    for g in range(tokens // 16):
        rows = slice(g * 16, g * 16 + 16)
        both = partial[rows] + part_in[rows, :]
        proj_ref[rows, :] = (both * (inverse[g] * multiplier)).astype(BF16)

    @pl.when(c != yh)
    def _():
        near.wait_recv()

    far[0].wait_recv()
    grad_ref[...] = (rs3_in[0] + rs3_in[1]) * (gain_col * multiplier)

    for copy in term_copies + hx_copies + [cx_copy, wy_far, part_copy]:
        copy.wait_send()

    @pl.when(c != yh)
    def _():
        wy_near.wait_send()
        far[0].wait_send()
        far[1].wait_send()

    @pl.when(c == yh)
    def _():
        near.wait_send()

    for d in range(1, n):
        ag1_copy(d).wait_send()
        rs2_copy(d).wait_send()
    for q, way, k in ag_slots:
        ag_copy(q, way, k).wait_send()
    for q, way, k in rs_slots:
        rs_copy(q, way, k)[1].wait_send()


def shards(
    replicas,
    n,
    delta_codes,
    scale_exponents,
    error_feedback,
    base_weights,
    outer_momentum,
    norm_gain,
    hidden_states,
    key_cotangent,
):
    tokens = hidden_states.shape[1]
    width = hidden_states.shape[2]
    half = width // 2
    h = n // 2
    any_space = pl.BlockSpec(memory_space=pl.ANY)
    vmem = pl.BlockSpec(memory_space=pltpu.VMEM)
    dma = pltpu.SemaphoreType.DMA
    rs_count = NQ * (2 * h - 1)
    ag_count = NG * (2 * h - 1)
    outs = pl.pallas_call(
        functools.partial(kernel, replicas, n, tokens),
        out_shape=(
            jax.ShapeDtypeStruct((tokens, LANES), BF16),
            jax.ShapeDtypeStruct((ROWS, LANES), F32),
            jax.ShapeDtypeStruct((ROWS, LANES), F32),
            jax.ShapeDtypeStruct((ROWS, LANES), F32),
        ),
        in_specs=[any_space] * 8,
        out_specs=(vmem,) * 4,
        scratch_shapes=[
            pltpu.VMEM((ROWS, LANES), jnp.int32),
            pltpu.VMEM((ROWS, LANES // BLOCK), jnp.int32),
            pltpu.VMEM((ROWS, LANES), F32),
            pltpu.VMEM((ROWS, LANES), F32),
            pltpu.VMEM((ROWS, LANES), F32),
            pltpu.VMEM((width // LANES, LANES), F32),
            pltpu.VMEM((tokens, LANES), BF16),
            pltpu.VMEM((2 * tokens, half), BF16),
            pltpu.VMEM((tokens, half), BF16),
            pltpu.VMEM((2 * tokens, LANES), BF16),
            pltpu.VMEM((replicas, ROWS, LANES), F32),
            pltpu.VMEM((ROWS, LANES), BF16),
            pltpu.VMEM((n, n, PAIR, LANES), BF16),
            pltpu.VMEM((n, n, PAIR, LANES), F32),
            pltpu.VMEM((PAIR, LANES), F32),
            pltpu.VMEM((rs_count, n // NQ, PAIR, LANES), BF16),
            pltpu.VMEM((rs_count, n // NQ, PAIR, LANES), BF16),
            pltpu.VMEM((n, PAIR, LANES), BF16),
            pltpu.VMEM((n, PAIR, LANES), BF16),
            pltpu.VMEM((2, ROWS, LANES), F32),
            pltpu.VMEM((2, ROWS, LANES), F32),
            pltpu.VMEM((tokens, LANES), F32),
            pltpu.VMEM((tokens, LANES), F32),
            dma((9,)),
            dma((replicas,)),
            dma((replicas,)),
            dma((NX,)),
            dma((NX,)),
            dma((2,)),
            dma((2,)),
            dma((2,)),
            dma((n,)),
            dma((n,)),
            dma((ag_count,)),
            dma((ag_count,)),
            dma((rs_count,)),
            dma((rs_count,)),
            dma((n,)),
            dma((n,)),
            dma((2,)),
            dma((2,)),
            dma((2,)),
        ],
        compiler_params=pltpu.CompilerParams(
            collective_id=0, has_side_effects=True, vmem_limit_bytes=40 * 1024 * 1024
        ),
        cost_estimate=pl.CostEstimate(
            flops=4 * tokens * width * LANES,
            bytes_accessed=2 * tokens * width,
            transcendentals=tokens,
        ),
    )(
        delta_codes[0],
        scale_exponents[0],
        error_feedback[0],
        base_weights,
        outer_momentum,
        norm_gain.reshape(width // LANES, LANES),
        hidden_states[0],
        key_cotangent[0],
    )
    projected, weight_grad, new_weights, new_momentum = outs
    return (projected[None], weight_grad[None], new_weights, new_momentum)


def solution(mesh):
    replicas = mesh.shape["replica"]
    n = math.isqrt(mesh.shape["fsdp"] // 4)
    return jax.shard_map(
        functools.partial(shards, replicas, n),
        mesh=mesh,
        in_specs=(
            P("replica", "fsdp", None),
            P("replica", "fsdp", None),
            P("replica", "fsdp", None),
            P("fsdp", None),
            P("fsdp", None),
            P(),
            P("replica", "fsdp", None),
            P("replica", "fsdp", None),
        ),
        out_specs=(
            P("replica", "fsdp", None),
            P("replica", "fsdp", None),
            P("fsdp", None),
            P("fsdp", None),
        ),
        check_vma=False,
    )
```

time: 1800 us -> 69.2 us (0.04)
  waiting for transfers between devices: 1750 us -> 0 us
  Pallas kernels: 0 us -> 58.5 us
    reduce_scatter x1 -> x0, waiting for transfers between devices: 1610 us -> none  [shards(): lax.psum_scatter(product * multiplier, 'fsdp', scatter_dimension=0, tiled...]
    all_gather x1 -> x0, waiting for transfers between devices: 137 us -> none  [shards(): lax.all_gather(weight_rows, 'fsdp', axis=0, tiled=True)]
    pallas_call x0 -> x1, Pallas kernels: none -> 58.5 us  [shards(): pl.pallas_call(functools.partial(kernel, replicas, n, tokens), out_shape=...]
  transfers between devices with their start and end apart: 2 -> 0, of which waited for: 2 -> 0; matrix products, arithmetic and copies ran while one was open for 1% -> 0% of each run, Pallas kernels for 0% -> 0%
where the time goes in v1:
time: 69.2 us; the launch traced here: 68.7 us
  Pallas kernels  58.5 us (85%)
  local copies, waits for them, and re-layouts  9.51 us (14%)
    pallas_call x1, Pallas kernels, shards(): pl.pallas_call(functools.partial(kernel, replicas, n, tokens), out_shape=...  58.5 us
    unnamed x18, local copies, waits for them, and re-layouts  8.75 us

profile of v1, /device:TPU:1, one launch (start us, length us, event | category | flops | bytes accessed | tf_op | source)
XLA Modules:
  0.0 68.7 jit_solution(10672459754653189259)
XLA Ops:
  0.6 0.8 %copy.12.exps_hbm = s32[32,4]{1,0:T(8,128)S(1)} copy(s32[32,4]{0,1:T(4,128)} %bitcast.15) | data formatting | bytes 1024 | tf_op jit(solution)/shard_map/squeeze | solution.py:580
  1.4 0.0 copy-start
  1.4 1.9 %copy-done = bf16[1,192,8192]{2,1,0:T(8,128)(2,1)S(1)} copy-done((bf16[1,192,8192]{2,1,0:T(8,128)(2,1)S(1)}, bf16[1,192,8192]{2,1,0:T(8,128)(2,1)}, u32[]{:S(2)}) %copy-start) | copy-done | bytes 3145752
  3.3 0.0 copy-start.1
  3.3 0.8 %copy-done.1 = bf16[1,192,128]{2,1,0:T(8,128)(2,1)S(1)} copy-done((bf16[1,192,128]{2,1,0:T(8,128)(2,1)S(1)}, bf16[1,192,128]{2,1,0:T(8,128)(2,1)}, u32[]{:S(2)}) %copy-start.1) | copy-done | bytes 49176
  4.1 0.0 copy-start.2
  4.1 0.8 %copy-done.2 = f32[8192]{0:T(1024)S(1)} copy-done((f32[8192]{0:T(1024)S(1)}, f32[8192]{0:T(1024)}, u32[]{:S(2)}) %copy-start.2) | copy-done | bytes 32792
  4.8 0.0 copy-start.3
  4.8 0.7 %copy-done.3 = s32[1,32,128]{2,1,0:T(8,128)S(1)} copy-done((s32[1,32,128]{2,1,0:T(8,128)S(1)}, s32[1,32,128]{2,1,0:T(8,128)}, u32[]{:S(2)}) %copy-start.3) | copy-done | bytes 16408
  5.6 0.0 copy-start.4
  5.6 0.7 %copy-done.4 = f32[1,32,128]{2,1,0:T(8,128)S(1)} copy-done((f32[1,32,128]{2,1,0:T(8,128)S(1)}, f32[1,32,128]{2,1,0:T(8,128)}, u32[]{:S(2)}) %copy-start.4) | copy-done | bytes 16408
  6.3 0.0 copy-start.5
  6.3 0.7 %copy-done.5 = f32[32,128]{1,0:T(8,128)S(1)} copy-done((f32[32,128]{1,0:T(8,128)S(1)}, f32[32,128]{1,0:T(8,128)}, u32[]{:S(2)}) %copy-start.5) | copy-done | bytes 16408
  7.0 0.0 copy-start.6
  7.0 0.7 %copy-done.6 = f32[32,128]{1,0:T(8,128)S(1)} copy-done((f32[32,128]{1,0:T(8,128)S(1)}, f32[32,128]{1,0:T(8,128)}, u32[]{:S(2)}) %copy-start.6) | copy-done | bytes 16408
  7.7 58.5 %shard_map.111 = (bf16[192,128]{1,0:T(8,128)(2,1)S(1)}, f32[32,128]{1,0:T(8,128)S(1)}, f32[32,128]{1,0:T(8,128)S(1)}, f32[32,128]{1,0:T(8,128)S(1)}) custom-call(s32[32,128]{1,0:T(8,128)S(1)} %bitcast.12, s32[32,4]{1,0:T(8,128)S(1)} %copy.12.exps_hbm, f32[32,128]{1,0:T(8,128)S(1)} %bitcast.13, f32[32,128]{1,0:T(8,128)S(1)} %copy-done.5, ...), custom_call_target="tpu_custom_call" | custom-call | flops 805306368 | bytes 3145728 | tf_op jit(solution)/shard_map/pallas_call | solution.py:516
  66.2 0.6 copy.17
  66.9 0.6 copy.18
  67.5 0.6 copy.19
  68.1 0.6 copy.20
Async XLA Ops:
  1.4 1.9 %copy-start = (bf16[1,192,8192]{2,1,0:T(8,128)(2,1)S(1)}, bf16[1,192,8192]{2,1,0:T(8,128)(2,1)}, u32[]{:S(2)}) copy-start(bf16[1,192,8192]{2,1,0:T(8,128)(2,1)} %param.14) | copy-start | bytes 9437188
  3.3 0.8 %copy-start.1 = (bf16[1,192,128]{2,1,0:T(8,128)(2,1)S(1)}, bf16[1,192,128]{2,1,0:T(8,128)(2,1)}, u32[]{:S(2)}) copy-start(bf16[1,192,128]{2,1,0:T(8,128)(2,1)} %param.15) | copy-start | bytes 147460
  4.1 0.8 %copy-start.2 = (f32[8192]{0:T(1024)S(1)}, f32[8192]{0:T(1024)}, u32[]{:S(2)}) copy-start(f32[8192]{0:T(1024)} %param.13) | copy-start | bytes 98308
  4.8 0.7 %copy-start.3 = (s32[1,32,128]{2,1,0:T(8,128)S(1)}, s32[1,32,128]{2,1,0:T(8,128)}, u32[]{:S(2)}) copy-start(s32[1,32,128]{2,1,0:T(8,128)} %param.8) | copy-start | bytes 49156
  5.6 0.7 %copy-start.4 = (f32[1,32,128]{2,1,0:T(8,128)S(1)}, f32[1,32,128]{2,1,0:T(8,128)}, u32[]{:S(2)}) copy-start(f32[1,32,128]{2,1,0:T(8,128)} %param.10) | copy-start | bytes 49156
  6.3 0.7 %copy-start.5 = (f32[32,128]{1,0:T(8,128)S(1)}, f32[32,128]{1,0:T(8,128)}, u32[]{:S(2)}) copy-start(f32[32,128]{1,0:T(8,128)} %base_hbm.1) | copy-start | bytes 49156
  7.0 0.7 %copy-start.6 = (f32[32,128]{1,0:T(8,128)S(1)}, f32[32,128]{1,0:T(8,128)}, u32[]{:S(2)}) copy-start(f32[32,128]{1,0:T(8,128)} %mom_hbm.1) | copy-start | bytes 49156

commit v2 on v1

v2 whole, which is shorter than its diff:
```python
import functools
import math

import jax
import jax.numpy as jnp
from jax import lax
from jax.experimental import pallas as pl
from jax.experimental.pallas import tpu as pltpu
from jax.sharding import PartitionSpec as P

BLOCK = 32
ROWS = 32
PAIR = 2 * ROWS
LANES = 128
NX = 4
VMEM_BYTES = 63 * 1024 * 1024
MESH = pl.DeviceIdType.MESH
BF16 = jnp.bfloat16
F32 = jnp.float32


def column(line, start):
    shape = (ROWS, line.shape[1])
    lane = lax.broadcasted_iota(jnp.int32, shape, 1)
    row = lax.broadcasted_iota(jnp.int32, shape, 0)
    return jnp.sum(jnp.where(lane == row + start, line, 0.0), axis=1, keepdims=True)


def decode(codes, exponents):
    powers = jnp.where(
        exponents == -6,
        2.0**-6,
        jnp.where(
            exponents == -5, 2.0**-5, jnp.where(exponents == -4, 2.0**-4, 2.0**-3)
        ),
    ).astype(F32)
    lane = lax.broadcasted_iota(jnp.int32, codes.shape, 1)
    scale = jnp.zeros(codes.shape, F32)
    for k in range(codes.shape[1] // BLOCK):
        scale = jnp.where(lane // BLOCK == k, column(powers[k : k + 1], 0), scale)
    magnitude_code = codes % 8
    level = magnitude_code // 2
    fraction = 0.5 * (magnitude_code % 2).astype(F32)
    magnitude = jnp.where(
        level == 0,
        fraction,
        jnp.where(level == 1, 1.0, jnp.where(level == 2, 2.0, 4.0)).astype(F32)
        * (1.0 + fraction),
    )
    return jnp.where(codes >= 8, -magnitude, magnitude) * scale


def ring_plan(n):
    if n == 8:
        return [1], 2, [3]
    if n == 4:
        return [], 1, []
    raise ValueError(n)


def kernel(
    replicas,
    n,
    tokens,
    codes_hbm,
    exps_hbm,
    err_hbm,
    base_hbm,
    mom_hbm,
    gain_hbm,
    hidden_hbm,
    cot_hbm,
    proj_ref,
    grad_ref,
    neww_ref,
    newm_ref,
    codes,
    exps,
    err,
    base,
    mom,
    gain,
    cot,
    hid,
    hother,
    cots,
    terms,
    share,
    shares,
    wh,
    prod,
    rs_out,
    rs_in,
    last_out,
    last_in,
    part_out,
    part_in,
    load_sem,
    term_send,
    term_recv,
    hx_send,
    hx_recv,
    cx_sem,
    share_send,
    share_recv,
    ag1_send,
    ag1_recv,
    ag2_send,
    ag2_recv,
    rs_send,
    rs_recv,
    last_send,
    last_recv,
    part_sem,
    ready_sem,
):
    half = n * n * PAIR
    h = n // 2
    direct, middle, further = ring_plan(n)
    model_width = 2 * half
    multiplier = 1.0 / math.sqrt(model_width)
    r = lax.axis_index("replica")
    index = lax.axis_index("fsdp")
    c = index % 2
    z = (index // 2) % n
    x = (index // (2 * n)) % n
    yh = index // (2 * n * n)
    me_a = (1 - c) * z + c * x
    me_b = (1 - c) * x + c * z

    def device(y_half, a, b, core):
        to_x = (1 - c) * b + c * a
        to_z = (1 - c) * a + c * b
        return (r, ((y_half * n + to_x) * n + to_z) * 2 + core)

    def on_column(step, y_half, core):
        return (lax.rem(r + step, replicas), ((y_half * n + x) * n + z) * 2 + core)

    def along_a(step):
        return device(yh, lax.rem(me_a + step + n, n), me_b, c)

    def along_b(step):
        return device(yh, me_a, lax.rem(me_b + step + n, n), c)

    sibling = on_column(0, yh, 1 - c)

    own = pl.ds(pl.multiple_of(c * half, half), half)
    others = pl.ds(pl.multiple_of((1 - c) * half, half), half)
    small = [
        (codes_hbm, codes),
        (exps_hbm, exps),
        (err_hbm, err),
        (base_hbm, base),
        (mom_hbm, mom),
        (gain_hbm, gain),
        (cot_hbm, cot),
    ]
    loads = [
        pltpu.make_async_copy(src, dst, load_sem.at[i])
        for i, (src, dst) in enumerate(small)
    ]
    load_own = pltpu.make_async_copy(
        hidden_hbm.at[:, own], hid.at[pl.ds(0, tokens)], load_sem.at[len(small)]
    )
    load_other = pltpu.make_async_copy(
        hidden_hbm.at[:, others], hother, load_sem.at[len(small) + 1]
    )

    barrier = pltpu.get_barrier_semaphore()
    partners = [on_column(0, 1 - yh, 0), on_column(0, 1 - yh, 1), sibling]
    for d in range(1, replicas):
        for y_half in range(2):
            for core in range(2):
                partners.append(on_column(d, y_half, core))
    partners += [along_a(d) for d in range(1, n)]
    partners += [along_b(d) for d in range(1, n)]
    for partner in partners:
        pl.semaphore_signal(barrier, inc=1, device_id=partner, device_id_type=MESH)
    for load in loads:
        load.start()
    load_own.start()
    load_other.start()

    for load in loads:
        load.wait()
    term = decode(codes[...], exps[...]) + err[...]
    terms[r] = term
    flat = index * ROWS
    gain_col = column(gain[pl.ds(flat // LANES, 1), :], lax.rem(flat, LANES))
    kept = (base[...] - (0.7 * 0.9 * 0.9) * mom[...]) * (1.0 / replicas)
    my_share = ((kept - (0.7 * 1.9 / replicas) * term) * gain_col).astype(BF16)
    share[...] = my_share

    pl.semaphore_wait(barrier, len(partners))

    def remote(src, dst, send, recv, to):
        return pltpu.make_async_remote_copy(
            src_ref=src,
            dst_ref=dst,
            send_sem=send,
            recv_sem=recv,
            device_id=to,
            device_id_type=MESH,
        )

    def share_copy(d, flip):
        y_half = (1 - yh) * flip + yh * (1 - flip)
        return remote(
            share,
            shares.at[r, c],
            share_send.at[d, flip],
            share_recv.at[r, c],
            on_column(d, y_half, yh),
        )

    share_spots = [(d, flip) for d in range(replicas) for flip in range(2)]
    for d, flip in share_spots[1:]:
        share_copy(d, flip).start()

    @pl.when(c != yh)
    def _():
        share_copy(0, 0).start()

    @pl.when(c == yh)
    def _():
        shares[r, c] = my_share

    hx_copies = []
    piece = tokens // NX
    for i in range(NX):
        copy = remote(
            hidden_hbm.at[pl.ds(i * piece, piece), others],
            hid.at[pl.ds(tokens + i * piece, piece)],
            hx_send.at[i],
            hx_recv.at[i],
            sibling,
        )
        copy.start()
        hx_copies.append(copy)
    term_copies = []
    for d in range(1, replicas):
        copy = remote(
            terms.at[r],
            terms.at[r],
            term_send.at[d],
            term_recv.at[d],
            on_column(d, yh, c),
        )
        copy.start()
        term_copies.append(copy)
    for d in range(1, n):
        pl.semaphore_signal(
            ready_sem, inc=1, device_id=along_b(d), device_id_type=MESH
        )

    load_own.wait()
    load_other.wait()
    inverse = []
    for g in range(tokens // 16):
        rows = pl.ds(g * 16, 16)
        square = jnp.zeros((16, LANES), F32)
        for ref in (hid, hother):
            for j in range(half // LANES):
                wide = ref[rows, j * LANES : (j + 1) * LANES].astype(F32)
                square = square + wide * wide
        mean = jnp.sum(square, axis=1, keepdims=True) * (1.0 / model_width)
        inv = lax.rsqrt(mean + 1e-05)
        inverse.append(inv)
        cots[rows, :] = (cot[rows, :].astype(F32) * inv).astype(BF16)
    cx_copy = remote(
        cots.at[pl.ds(0, tokens)],
        cots.at[pl.ds(tokens, tokens)],
        cx_sem.at[0],
        cx_sem.at[1],
        sibling,
    )
    cx_copy.start()

    for copy in hx_copies:
        copy.wait_recv()
    cx_copy.wait_recv()
    cots_t = cots[...].T
    my_pair = me_a // 2

    def products(offset):
        p = lax.rem(my_pair + offset, h)
        for j in range(0, n, 2):
            tiles = []
            for t in (j, j + 1):
                at = (1 - c) * (t * n * PAIR + p * LANES) + c * (
                    p * 2 * n * PAIR + t * LANES
                )
                tiles.append(hid[:, pl.ds(pl.multiple_of(at, LANES), LANES)])
            out = jnp.dot(
                cots_t,
                jnp.concatenate(tiles, axis=1),
                preferred_element_type=F32,
            ).T
            for i, t in enumerate((j, j + 1)):
                for s in range(2):
                    a = 2 * p + (1 - c) * s + c * (t // h)
                    b = (1 - c) * t + c * (2 * (t % h) + s)
                    start = i * LANES + s * PAIR
                    prod[a, b] = out[start : start + PAIR]

    order = sorted(range(n), key=lambda d: -min(d, n - d))
    groups = [order[:h], order[h:]]
    ways = (1, -1)
    rs_slots = {}
    for q in range(2):
        if middle < h:
            rs_slots["far", q, ways[q], h] = len(rs_slots)
        for s in ways:
            for d in further:
                rs_slots["far", q, s, d] = len(rs_slots)
    for q in range(2):
        for s in ways:
            for d in [middle] + direct:
                rs_slots["near", q, s, d] = len(rs_slots)

    def rs_copy(key):
        kind, _, s, d = key
        slot = rs_slots[key]
        return remote(
            rs_out.at[slot],
            rs_in.at[slot],
            rs_send.at[slot],
            rs_recv.at[slot],
            along_a(s * (d - middle) if kind == "far" else s * d),
        )

    def rs_send_block(key):
        kind, q, s, d = key
        to = lax.rem(me_a + s * d + n, n)
        arrived = []
        if kind == "near" and d == middle:
            arrived = [k for k in rs_slots if k[0] == "far" and k[1:3] == (q, s)]
            for k in arrived:
                rs_copy(k).wait_recv()
        for i, e in enumerate(groups[q]):
            value = prod[to, lax.rem(me_b + e, n)]
            for k in arrived:
                value = value + rs_in[rs_slots[k], i].astype(F32)
            rs_out[rs_slots[key], i] = value.astype(BF16)
        rs_copy(key).start()

    def rs_sends(kind, distances):
        for key in rs_slots:
            if key[0] == kind and key[3] in distances:
                rs_send_block(key)

    def last_copy(e, core):
        return remote(
            last_out.at[e, core],
            last_in.at[yh, e],
            last_send.at[e, core],
            last_recv.at[yh, e],
            device(c, me_a, lax.rem(me_b + e, n), core),
        )

    def rs_last(q):
        keys = [k for k in rs_slots if k[0] == "near" and k[1] == q]
        for k in keys:
            rs_copy(k).wait_recv()
        for i, e in enumerate(groups[q]):
            value = prod[me_a, lax.rem(me_b + e, n)]
            for k in keys:
                value = value + rs_in[rs_slots[k], i].astype(F32)
            value = value.astype(BF16)
            last_out[e, 0] = value[:ROWS]
            last_out[e, 1] = value[ROWS:]
            if e > 0:
                last_copy(e, 0).start()
                last_copy(e, 1).start()
            else:

                @pl.when(c != yh)
                def _():
                    last_copy(0, 0).start()
                    last_copy(0, 1).start()

                @pl.when(c == yh)
                def _():
                    last_copy(0, 1 - c).start()
                    last_in[yh, 0] = last_out[0, c]

    def last_wait(y_half, e):
        spot = last_in.at[y_half, e]
        remote(
            last_out.at[0, 0],
            spot,
            last_send.at[0, 0],
            last_recv.at[y_half, e],
            sibling,
        ).wait_recv()

    nearest = order[::-1]
    place = {d: i for i, d in enumerate(nearest)}

    def ag1_copy(d):
        return remote(
            wh.at[0, 0],
            wh.at[0, place[n - d]],
            ag1_send.at[d],
            ag1_recv.at[d],
            along_a(d),
        )

    ag_slots = {}
    for g in range(2):
        for s in ways:
            for d in [middle] + direct:
                ag_slots["near", g, s, d] = len(ag_slots)
        for s in ways:
            for d in further + [h]:
                ag_slots["far", g, s, d] = len(ag_slots)

    def ag_copy(key):
        kind, g, s, d = key
        first, count = g * h, h
        if d == h:
            count = h // 2
            first += count * (s < 0)
        blocks = pl.ds(first, count)
        came, hops = (0, d) if kind == "near" else (middle, d - middle)
        slot = ag_slots[key]
        return remote(
            wh.at[(-s * came) % n, blocks],
            wh.at[(-s * d) % n, blocks],
            ag2_send.at[slot],
            ag2_recv.at[slot],
            along_b(s * hops),
        )

    def ag_near(g):
        for d in nearest[g * h : (g + 1) * h]:
            if d > 0:
                ag1_copy(n - d).wait_recv()
        for key in ag_slots:
            if key[:2] == ("near", g):
                ag_copy(key).start()

    def ag_far(g):
        for s in ways:
            ag_copy(("near", g, s, middle)).wait_recv()
            for d in further + [h]:
                ag_copy(("far", g, s, d)).start()

    pairs = sorted(range(h), key=lambda d: -min(d, h - d))
    for offset in pairs[:-1]:
        products(offset)
    rs_sends("far", [h])
    rs_sends("far", further)
    products(pairs[-1])

    @pl.when(c != yh)
    def _():
        remote(
            share, shares.at[r, c], share_send.at[0, 0], share_recv.at[r, c], sibling
        ).wait_recv()

    for d in range(replicas):
        for other in range(2):
            if (d, other) != (0, 0):
                source = lax.rem(r + d, replicas)
                core = (c + other) % 2
                remote(
                    share,
                    shares.at[source, core],
                    share_send.at[0, 0],
                    share_recv.at[source, core],
                    sibling,
                ).wait_recv()
    for core in range(2):
        rows64 = shares[0, core].astype(F32)
        for d in range(1, replicas):
            rows64 = rows64 + shares[d, core].astype(F32)
        wh[0, 0, pl.ds(core * ROWS, ROWS)] = rows64.astype(BF16)
    for d in nearest[1:]:
        ag1_copy(d).start()

    rs_sends("near", direct)
    ag_near(0)
    rs_sends("near", [middle])
    ag_near(1)
    ag_far(0)

    for copy in term_copies:
        copy.wait_recv()
    summed = terms[0]
    for d in range(1, replicas):
        summed = summed + terms[d]
    outer_grad = summed / replicas
    new_momentum = 0.9 * mom[...] + outer_grad
    newm_ref[...] = new_momentum
    neww_ref[...] = base[...] - 0.7 * (outer_grad + 0.9 * new_momentum)

    pl.semaphore_wait(ready_sem, n - 1)
    rs_last(0)
    rs_last(1)
    ag_far(1)
    for key in ag_slots:
        if key[0] == "far" or key[3] != middle:
            ag_copy(key).wait_recv()

    pieces = []
    for tx in range(n):
        for tz in range(n):
            a = (1 - c) * tz + c * tx
            b = (1 - c) * tx + c * tz
            rel_a = lax.rem(a - me_a + n, n)
            rel_b = lax.rem(b - me_b + n, n)
            pieces.append((rel_b, rel_a))
    tiles = []
    for rel_b, rel_a in pieces:
        back = rel_a // h
        at = (1 - back) * 2 * rel_a + back * (2 * (n - rel_a) - 1)
        tiles.append(wh[rel_b, at])
    partial = jnp.dot(
        hid[...], jnp.concatenate(tiles, axis=0), preferred_element_type=F32
    )
    part_out[...] = partial[tokens:]
    part_copy = remote(part_out, part_in, part_sem.at[0], part_sem.at[1], sibling)
    part_copy.start()

    @pl.when(c != yh)
    def _():
        last_wait(yh, 0)

    last_wait(1 - yh, 0)
    for e in range(1, n):
        last_wait(0, e)
        last_wait(1, e)
    grad = jnp.zeros((ROWS, LANES), F32)
    for y_half in range(2):
        for e in range(n):
            grad = grad + last_in[y_half, e].astype(F32)
    grad_ref[...] = grad * (gain_col * multiplier)

    part_copy.wait_recv()
    for g in range(tokens // 16):
        rows = slice(g * 16, g * 16 + 16)
        both = partial[rows] + part_in[rows, :]
        proj_ref[rows, :] = (both * (inverse[g] * multiplier)).astype(BF16)

    for copy in term_copies + hx_copies + [cx_copy, part_copy]:
        copy.wait_send()
    for d, flip in share_spots[1:]:
        share_copy(d, flip).wait_send()

    @pl.when(c != yh)
    def _():
        share_copy(0, 0).wait_send()
        last_copy(0, 0).wait_send()
        last_copy(0, 1).wait_send()

    @pl.when(c == yh)
    def _():
        last_copy(0, 1 - c).wait_send()

    for d in range(1, n):
        ag1_copy(d).wait_send()
        last_copy(d, 0).wait_send()
        last_copy(d, 1).wait_send()
    for key in ag_slots:
        ag_copy(key).wait_send()
    for key in rs_slots:
        rs_copy(key).wait_send()


def deliver(*refs):
    count = (len(refs) - 1) // 2
    copies = [
        pltpu.make_async_copy(refs[i], refs[count + i], refs[-1].at[i])
        for i in range(count)
    ]
    for copy in copies:
        copy.start()
    for copy in copies:
        copy.wait()


def shards(
    replicas,
    n,
    delta_codes,
    scale_exponents,
    error_feedback,
    base_weights,
    outer_momentum,
    norm_gain,
    hidden_states,
    key_cotangent,
):
    tokens = hidden_states.shape[1]
    width = hidden_states.shape[2]
    half = width // 2
    h = n // 2
    hbm = pl.BlockSpec(memory_space=pltpu.HBM)
    dma = pltpu.SemaphoreType.DMA
    rs_count = 14 if n == 8 else 6
    ag_count = 16 if n == 8 else 8
    outs = pl.pallas_call(
        functools.partial(kernel, replicas, n, tokens),
        out_shape=(
            pltpu.VMEM((tokens, LANES), BF16),
            pltpu.VMEM((ROWS, LANES), F32),
            pltpu.VMEM((ROWS, LANES), F32),
            pltpu.VMEM((ROWS, LANES), F32),
        ),
        in_specs=[hbm] * 8,
        out_specs=(pl.BlockSpec(memory_space=pltpu.VMEM),) * 4,
        scratch_shapes=[
            pltpu.VMEM((ROWS, LANES), jnp.int32),
            pltpu.VMEM((LANES // BLOCK, ROWS), jnp.int32),
            pltpu.VMEM((ROWS, LANES), F32),
            pltpu.VMEM((ROWS, LANES), F32),
            pltpu.VMEM((ROWS, LANES), F32),
            pltpu.VMEM((width // LANES, LANES), F32),
            pltpu.VMEM((tokens, LANES), BF16),
            pltpu.VMEM((2 * tokens, half), BF16),
            pltpu.VMEM((tokens, half), BF16),
            pltpu.VMEM((2 * tokens, LANES), BF16),
            pltpu.VMEM((replicas, ROWS, LANES), F32),
            pltpu.VMEM((ROWS, LANES), BF16),
            pltpu.VMEM((replicas, 2, ROWS, LANES), BF16),
            pltpu.VMEM((n, n, PAIR, LANES), BF16),
            pltpu.VMEM((n, n, PAIR, LANES), F32),
            pltpu.VMEM((rs_count, h, PAIR, LANES), BF16),
            pltpu.VMEM((rs_count, h, PAIR, LANES), BF16),
            pltpu.VMEM((n, 2, ROWS, LANES), BF16),
            pltpu.VMEM((2, n, ROWS, LANES), BF16),
            pltpu.VMEM((tokens, LANES), F32),
            pltpu.VMEM((tokens, LANES), F32),
            dma((9,)),
            dma((replicas,)),
            dma((replicas,)),
            dma((NX,)),
            dma((NX,)),
            dma((2,)),
            dma((replicas, 2)),
            dma((replicas, 2)),
            dma((n,)),
            dma((n,)),
            dma((ag_count,)),
            dma((ag_count,)),
            dma((rs_count,)),
            dma((rs_count,)),
            dma((n, 2)),
            dma((2, n)),
            dma((2,)),
            pltpu.SemaphoreType.REGULAR,
        ],
        compiler_params=pltpu.CompilerParams(
            collective_id=0, has_side_effects=True, vmem_limit_bytes=VMEM_BYTES
        ),
        cost_estimate=pl.CostEstimate(
            flops=4 * tokens * width * LANES,
            bytes_accessed=2 * tokens * width,
            transcendentals=tokens,
        ),
    )(
        delta_codes[0],
        scale_exponents[0].T,
        error_feedback[0],
        base_weights,
        outer_momentum,
        norm_gain.reshape(width // LANES, LANES),
        hidden_states[0],
        key_cotangent[0],
    )
    projected, weight_grad, new_weights, new_momentum = pl.pallas_call(
        deliver,
        out_shape=tuple(jax.ShapeDtypeStruct(o.shape, o.dtype) for o in outs),
        in_specs=[pl.BlockSpec(memory_space=pl.ANY)] * 4,
        out_specs=(hbm,) * 4,
        scratch_shapes=[dma((4,))],
    )(*outs)
    return (projected[None], weight_grad[None], new_weights, new_momentum)


def solution(mesh):
    replicas = mesh.shape["replica"]
    n = math.isqrt(mesh.shape["fsdp"] // 4)
    return jax.shard_map(
        functools.partial(shards, replicas, n),
        mesh=mesh,
        in_specs=(
            P("replica", "fsdp", None),
            P("replica", "fsdp", None),
            P("replica", "fsdp", None),
            P("fsdp", None),
            P("fsdp", None),
            P(),
            P("replica", "fsdp", None),
            P("replica", "fsdp", None),
        ),
        out_specs=(
            P("replica", "fsdp", None),
            P("replica", "fsdp", None),
            P("fsdp", None),
            P("fsdp", None),
        ),
        check_vma=False,
    )
```

time: 69.2 us -> 58.7 us (0.85)
  local copies, waits for them, and re-layouts: 9.51 us -> 2.41 us
  Pallas kernels: 58.5 us -> 55.4 us
    pallas_call x1, Pallas kernels: 58.5 us -> 51.3 us  [shards(): pl.pallas_call(functools.partial(kernel, replicas, n, tokens), out_shape=...]
    unnamed x18 -> x8, local copies, waits for them, and re-layouts: 8.75 us -> 2.41 us
    pallas_call x0 -> x1, Pallas kernels: none -> 4.11 us  [shards(): pl.pallas_call(deliver, out_shape=tuple((jax.ShapeDtypeStruct(o.shape, o....]
    squeeze x1 -> x0, local copies, waits for them, and re-layouts: 0.76 us -> none  [shards(): scale_exponents[0]]
where the time goes in v2:
time: 58.7 us; the launch traced here: 58.5 us
  Pallas kernels  55.4 us (94%)
  local copies, waits for them, and re-layouts  2.41 us (4%)
  between operations  0.65 us (1%)
    pallas_call x1, Pallas kernels, shards(): pl.pallas_call(functools.partial(kernel, replicas, n, tokens), out_shape=...  51.3 us
    pallas_call x1, Pallas kernels, shards(): pl.pallas_call(deliver, out_shape=tuple((jax.ShapeDtypeStruct(o.shape, o....  4.11 us
    unnamed x8, local copies, waits for them, and re-layouts  2.41 us

profile of v2, /device:TPU:1, one launch (start us, length us, event | category | flops | bytes accessed | tf_op | source)
XLA Modules:
  0.0 58.5 jit_solution(10982138814335603481)
XLA Ops:
  0.6 51.3 %shard_map.111 = (bf16[192,128]{1,0:T(8,128)(2,1)S(1)}, f32[32,128]{1,0:T(8,128)S(1)}, f32[32,128]{1,0:T(8,128)S(1)}, f32[32,128]{1,0:T(8,128)S(1)}) custom-call(s32[32,128]{1,0:T(8,128)} %bitcast.13, s32[4,32]{1,0:T(4,128)} %bitcast.15, f32[32,128]{1,0:T(8,128)} %bitcast.14, f32[32,128]{1,0:T(8,128)} %base_hbm.1, f32[32,128]{1,0:T(8,128)} %mom_hbm.1, ...), custom_call_target="tpu_custom_call" | custom-call | flops 805306368 | bytes 3145728 | tf_op jit(solution)/shard_map/pallas_call | solution.py:603
  52.0 0.0 copy-start
  52.0 0.6 %copy-done = bf16[192,128]{1,0:T(8,128)(2,1)} copy-done((bf16[192,128]{1,0:T(8,128)(2,1)}, bf16[192,128]{1,0:T(8,128)(2,1)S(1)}, u32[]{:S(2)}) %copy-start) | copy-done | bytes 49176
  52.6 0.0 copy-start.1
  52.6 0.6 %copy-done.1 = f32[32,128]{1,0:T(8,128)} copy-done((f32[32,128]{1,0:T(8,128)}, f32[32,128]{1,0:T(8,128)S(1)}, u32[]{:S(2)}) %copy-start.1) | copy-done | bytes 16408
  53.2 0.0 copy-start.2
  53.2 0.6 %copy-done.2 = f32[32,128]{1,0:T(8,128)} copy-done((f32[32,128]{1,0:T(8,128)}, f32[32,128]{1,0:T(8,128)S(1)}, u32[]{:S(2)}) %copy-start.2) | copy-done | bytes 16408
  53.8 0.0 copy-start.3
  53.8 0.6 %copy-done.3 = f32[32,128]{1,0:T(8,128)} copy-done((f32[32,128]{1,0:T(8,128)}, f32[32,128]{1,0:T(8,128)S(1)}, u32[]{:S(2)}) %copy-start.3) | copy-done | bytes 16408
  54.4 4.1 %shard_map.112 = (bf16[192,128]{1,0:T(8,128)(2,1)}, f32[32,128]{1,0:T(8,128)}, f32[32,128]{1,0:T(8,128)}, f32[32,128]{1,0:T(8,128)}) custom-call(bf16[192,128]{1,0:T(8,128)(2,1)} %copy-done, f32[32,128]{1,0:T(8,128)} %copy-done.1, f32[32,128]{1,0:T(8,128)} %copy-done.2, f32[32,128]{1,0:T(8,128)} %copy-done.3), custom_call_target="tpu_custom_call" | custom-call | tf_op jit(solution)/shard_map/pallas_call | solution.py:672
Async XLA Ops:
  52.0 0.6 %copy-start = (bf16[192,128]{1,0:T(8,128)(2,1)}, bf16[192,128]{1,0:T(8,128)(2,1)S(1)}, u32[]{:S(2)}) copy-start(bf16[192,128]{1,0:T(8,128)(2,1)S(1)} %get-tuple-element.12.refs_0_) | copy-start | bytes 147460
  52.6 0.6 %copy-start.1 = (f32[32,128]{1,0:T(8,128)}, f32[32,128]{1,0:T(8,128)S(1)}, u32[]{:S(2)}) copy-start(f32[32,128]{1,0:T(8,128)S(1)} %get-tuple-element.13.refs_1_) | copy-start | bytes 49156
  53.2 0.6 %copy-start.2 = (f32[32,128]{1,0:T(8,128)}, f32[32,128]{1,0:T(8,128)S(1)}, u32[]{:S(2)}) copy-start(f32[32,128]{1,0:T(8,128)S(1)} %get-tuple-element.14.refs_2_) | copy-start | bytes 49156
  53.8 0.6 %copy-start.3 = (f32[32,128]{1,0:T(8,128)}, f32[32,128]{1,0:T(8,128)S(1)}, u32[]{:S(2)}) copy-start(f32[32,128]{1,0:T(8,128)S(1)} %get-tuple-element.15.refs_3_) | copy-start | bytes 49156

commit v3 on v2

--- a/solution.py
+++ b/solution.py
@@ -14,6 +14,7 @@
 LANES = 128
 NX = 4
 VMEM_BYTES = 63 * 1024 * 1024
+SMALL_BYTES = 4 * 1024 * 1024
 MESH = pl.DeviceIdType.MESH
 BF16 = jnp.bfloat16
 F32 = jnp.float32
@@ -675,6 +676,7 @@
         in_specs=[pl.BlockSpec(memory_space=pl.ANY)] * 4,
         out_specs=(hbm,) * 4,
         scratch_shapes=[dma((4,))],
+        compiler_params=pltpu.CompilerParams(vmem_limit_bytes=SMALL_BYTES),
     )(*outs)
     return (projected[None], weight_grad[None], new_weights, new_momentum)
 

time: 58.7 us -> 52.8 us (0.90)
  Pallas kernels: 55.4 us -> 52 us
  local copies, waits for them, and re-layouts: 2.41 us -> 0 us
    pallas_call x1, Pallas kernels: 4.11 us -> 0.67 us  [shards(): pl.pallas_call(deliver, out_shape=tuple((jax.ShapeDtypeStruct(o.shape, o....]
    unnamed x8 -> x0, local copies, waits for them, and re-layouts: 2.41 us -> none
where the time goes in v3:
time: 52.8 us; the launch traced here: 52.6 us
  Pallas kernels  52 us (98%)
  between operations  0.64 us (1%)
    pallas_call x1, Pallas kernels, shards(): pl.pallas_call(functools.partial(kernel, replicas, n, tokens), out_shape=...  51.3 us

profile of v3, /device:TPU:1, one launch (start us, length us, event | category | flops | bytes accessed | tf_op | source)
XLA Modules:
  0.0 52.6 jit_solution(14174170819384696295)
XLA Ops:
  0.6 51.3 %shard_map.111 = (bf16[192,128]{1,0:T(8,128)(2,1)S(1)}, f32[32,128]{1,0:T(8,128)S(1)}, f32[32,128]{1,0:T(8,128)S(1)}, f32[32,128]{1,0:T(8,128)S(1)}) custom-call(s32[32,128]{1,0:T(8,128)} %bitcast.13, s32[4,32]{1,0:T(4,128)} %bitcast.15, f32[32,128]{1,0:T(8,128)} %bitcast.14, f32[32,128]{1,0:T(8,128)} %base_hbm.1, f32[32,128]{1,0:T(8,128)} %mom_hbm.1, ...), custom_call_target="tpu_custom_call" | custom-call | flops 805306368 | bytes 3145728 | tf_op jit(solution)/shard_map/pallas_call | solution.py:604
  52.0 0.7 %shard_map.112 = (bf16[192,128]{1,0:T(8,128)(2,1)}, f32[32,128]{1,0:T(8,128)}, f32[32,128]{1,0:T(8,128)}, f32[32,128]{1,0:T(8,128)}) custom-call(bf16[192,128]{1,0:T(8,128)(2,1)S(1)} %get-tuple-element.12.refs_0_, f32[32,128]{1,0:T(8,128)S(1)} %get-tuple-element.13.refs_1_, f32[32,128]{1,0:T(8,128)S(1)} %get-tuple-element.14.refs_2_, ...), custom_call_target="tpu_custom_call" | custom-call | tf_op jit(solution)/shard_map/pallas_call | solution.py:673

commit v4 on v3

--- a/solution.py
+++ b/solution.py
@@ -480,10 +480,10 @@
     for d in nearest[1:]:
         ag1_copy(d).start()
 
-    rs_sends("near", direct)
     ag_near(0)
     rs_sends("near", [middle])
     ag_near(1)
+    rs_sends("near", direct)
     ag_far(0)
 
     for copy in term_copies:

time: 52.8 us -> 55.7 us (1.055)
  Pallas kernels: 52 us -> 54.8 us
    pallas_call x1, Pallas kernels: 51.3 us -> 54.2 us  [shards(): pl.pallas_call(functools.partial(kernel, replicas, n, tokens), out_shape=...]
where the time goes in v4:
time: 55.7 us; the launch traced here: 55.5 us
  Pallas kernels  54.8 us (98%)
  between operations  0.64 us (1%)
    pallas_call x1, Pallas kernels, shards(): pl.pallas_call(functools.partial(kernel, replicas, n, tokens), out_shape=...  54.2 us

profile of v4, /device:TPU:1, one launch (start us, length us, event | category | flops | bytes accessed | tf_op | source)
XLA Modules:
  0.0 55.5 jit_solution(3029004495296894806)
XLA Ops:
  0.6 54.2 %shard_map.111 = (bf16[192,128]{1,0:T(8,128)(2,1)S(1)}, f32[32,128]{1,0:T(8,128)S(1)}, f32[32,128]{1,0:T(8,128)S(1)}, f32[32,128]{1,0:T(8,128)S(1)}) custom-call(s32[32,128]{1,0:T(8,128)} %bitcast.13, s32[4,32]{1,0:T(4,128)} %bitcast.15, f32[32,128]{1,0:T(8,128)} %bitcast.14, f32[32,128]{1,0:T(8,128)} %base_hbm.1, f32[32,128]{1,0:T(8,128)} %mom_hbm.1, ...), custom_call_target="tpu_custom_call" | custom-call | flops 805306368 | bytes 3145728 | tf_op jit(solution)/shard_map/pallas_call | solution.py:604
  54.8 0.7 %shard_map.112 = (bf16[192,128]{1,0:T(8,128)(2,1)}, f32[32,128]{1,0:T(8,128)}, f32[32,128]{1,0:T(8,128)}, f32[32,128]{1,0:T(8,128)}) custom-call(bf16[192,128]{1,0:T(8,128)(2,1)S(1)} %get-tuple-element.12.refs_0_, f32[32,128]{1,0:T(8,128)S(1)} %get-tuple-element.13.refs_1_, f32[32,128]{1,0:T(8,128)S(1)} %get-tuple-element.14.refs_2_, ...), custom_call_target="tpu_custom_call" | custom-call | tf_op jit(solution)/shard_map/pallas_call | solution.py:673
